TPU v7x, 256 devices: a whole 4x4x8 slice. The times are simulated.
256 devices in a mesh: ctx: 64 (over z, x, core), head: 4 (over y).
Axes of the slice: x: 4, y: 4, z: 8, core: 2. Of those that a mesh axis runs over, the one named last changes fastest.
Arguments:
- activations: bfloat16 [8192, 8192], P('ctx', 'head'), may hold values from -6 to 6
- adapter_down: bfloat16 [8192, 768], P('head'), may hold values from -0.0625 to 0.0625
- adapter_ids: int32 [8192, 2], P('ctx'), may hold values from 0 to 7, all different within a row
- adapter_weight: float32 [8192, 2], P('ctx'), may hold values from 0.05 to 0.95, as said below
- query_base: bfloat16 [8192, 8192], P('ctx', 'head'), may hold values from -110 to 110
- key_base: bfloat16 [8192, 1024], P('ctx', 'head'), may hold values from -6 to 6
- value_base: bfloat16 [8192, 1024], P('ctx', 'head'), may hold values from -6 to 6
- up_query: bfloat16 [256, 8192], P(None, 'head'), may hold values from -1 to 1
- up_key: bfloat16 [256, 1024], P(None, 'head'), may hold values from -1 to 1
- up_value: bfloat16 [256, 1024], P(None, 'head'), may hold values from -1 to 1
Outputs:
- attended: bfloat16 [8192, 8192], P('ctx', 'head')
Inputs may be any that keep to these rules, and one draw needn't show every extreme that they name: `adapter_weight`: each row holds two weights that sum to one, the first the larger.
All inputs are finite; a program needn't handle non-finite values.
Results may differ from a plain program's by a relative error of at most 0.029.
Values may be sent and summed in bfloat16 or wider, within the bound.
No kernel may reach another device: no remote copies, remote signals or barrier semaphores. Data moves between devices by JAX's collectives and lax.ppermute only.
A program may use at most 64 MiB of HBM per device.

v0:
```python
import math

import jax
import jax.numpy as jnp
from jax import lax
from jax.sharding import PartitionSpec as P

HD = 128
ADAPTERS = 8
RANK = 32


rope_base = 500000.0
floor_value = -1e30


def rotate(values, positions):
    row_count = values.shape[0]
    heads = values.shape[1] // HD
    half_width = HD // 2
    inverse = jnp.exp(jnp.arange(half_width, dtype=jnp.float32) * (-2.0 * math.log(rope_base) / HD))
    angles = positions.astype(jnp.float32)[:, None] * inverse[None, :]
    cosine = jnp.cos(angles)[:, None, :]
    sine = jnp.sin(angles)[:, None, :]
    shaped = values.reshape(row_count, heads, HD)
    first_half = shaped[:, :, :half_width]
    second_half = shaped[:, :, half_width:]
    turned = jnp.concatenate(
        [first_half * cosine - second_half * sine, second_half * cosine + first_half * sine], axis=2
    )
    return turned.reshape(row_count, heads * HD)


def mixture(adapter_ids, adapter_weight):
    labels = jnp.arange(ADAPTERS, dtype=jnp.int32)
    matches = (adapter_ids[:, :, None] == labels[None, None, :]).astype(jnp.float32)
    return jnp.sum(matches * adapter_weight[:, :, None], axis=1)


def gate_rows(low_rank, coefficient):
    row_count = low_rank.shape[0]
    shaped = low_rank.reshape(row_count, 3, ADAPTERS, RANK)
    gated = shaped * coefficient[:, None, :, None]
    return gated.astype(jnp.bfloat16).reshape(row_count, 3 * ADAPTERS * RANK)


def project(gated, query_base, key_base, value_base, up_query, up_key, up_value, positions):
    span = ADAPTERS * RANK
    query_raw = query_base.astype(jnp.float32) + jnp.dot(
        gated[:, :span], up_query, preferred_element_type=jnp.float32
    )
    key_raw = key_base.astype(jnp.float32) + jnp.dot(
        gated[:, span : 2 * span], up_key, preferred_element_type=jnp.float32
    )
    value_raw = value_base.astype(jnp.float32) + jnp.dot(
        gated[:, 2 * span :], up_value, preferred_element_type=jnp.float32
    )
    query = rotate(query_raw, positions).astype(jnp.bfloat16)
    keys = rotate(key_raw, positions).astype(jnp.bfloat16)
    return (query, keys, value_raw.astype(jnp.bfloat16))


def arrange(rows, local_kv, group_size):
    row_count = rows.shape[0]
    shaped = rows.reshape(row_count, local_kv, group_size, HD).transpose(1, 2, 0, 3)
    return shaped.reshape(local_kv, group_size * row_count, HD)


def restore(partial_value, local_kv, group_size, row_count):
    top_score, total, accum = partial_value
    normed = accum / total[:, :, None]
    shaped = normed.reshape(local_kv, group_size, row_count, HD).transpose(2, 0, 1, 3)
    return shaped.reshape(row_count, local_kv * group_size * HD).astype(jnp.bfloat16)


def on_device(
    activations,
    adapter_down,
    adapter_ids,
    adapter_weight,
    query_base,
    key_base,
    value_base,
    up_query,
    up_key,
    up_value,
):
    row_count = activations.shape[0]
    partial_low = jnp.dot(activations, adapter_down, preferred_element_type=jnp.float32)
    coefficient = mixture(adapter_ids, adapter_weight)
    low_rank = lax.psum(partial_low, "head")
    gated = gate_rows(low_rank, coefficient)
    positions = lax.axis_index("ctx") * row_count + jnp.arange(row_count, dtype=jnp.int32)
    query, keys, values = project(
        gated, query_base, key_base, value_base, up_query, up_key, up_value, positions
    )
    local_kv = keys.shape[1] // HD
    group_size = query.shape[1] // HD // local_kv
    half_rows = row_count // 2
    scale_factor = 1.0 / math.sqrt(HD)
    early_query = query[:half_rows]
    early_pos = positions[:half_rows]
    late_query = query[half_rows:]
    late_pos = positions[half_rows:]
    groups = (
        (arrange(early_query, local_kv, group_size), jnp.tile(early_pos, group_size)),
        (arrange(late_query, local_kv, group_size), jnp.tile(late_pos, group_size)),
    )
    group_rows = group_size * half_rows
    start_state = tuple(
        (
            (
                jnp.full((local_kv, group_rows), floor_value, jnp.float32),
                jnp.zeros((local_kv, group_rows), jnp.float32),
                jnp.zeros((local_kv, group_rows, HD), jnp.float32),
            )
            for entry in groups
        )
    )
    key_piece = lax.all_gather(keys, "ctx", axis=0, tiled=True)
    value_piece = lax.all_gather(values, "ctx", axis=0, tiled=True)
    piece_rows = key_piece.shape[0]
    step_rows = math.gcd(piece_rows, 512)
    step_count = piece_rows // step_rows
    key_steps = key_piece.reshape(step_count, step_rows, local_kv, HD)
    value_steps = value_piece.reshape(step_count, step_rows, local_kv, HD)

    def one_step(running, operands):
        key_block, value_block, step_index = operands
        block_start = step_index * step_rows
        key_pos = block_start + jnp.arange(step_rows, dtype=jnp.int32)
        updated = []
        for entry, partial_value in zip(groups, running):
            query_rows, query_pos = entry

            def compute(previous, query_rows=query_rows, query_pos=query_pos):
                old_top, old_total, old_accum = previous
                scores = (
                    jnp.einsum(
                        "gqd,kgd->gqk", query_rows, key_block, preferred_element_type=jnp.float32
                    )
                    * scale_factor
                )
                allowed = (query_pos[:, None] >= key_pos[None, :])[None]
                scores = jnp.where(allowed, scores, floor_value)
                new_top = jnp.maximum(old_top, jnp.max(scores, axis=2))
                shrink = jnp.exp(old_top - new_top)
                expo = jnp.where(allowed, jnp.exp(scores - new_top[:, :, None]), 0.0)
                new_total = old_total * shrink + jnp.sum(expo, axis=2)
                summed = jnp.einsum(
                    "gqk,kgd->gqd",
                    expo.astype(jnp.bfloat16),
                    value_block,
                    preferred_element_type=jnp.float32,
                )
                return (new_top, new_total, old_accum * shrink[:, :, None] + summed)

            def unchanged(previous):
                return previous

            updated.append(
                lax.cond(block_start <= jnp.max(query_pos), compute, unchanged, partial_value)
            )
        return (tuple(updated), None)

    outcome, unused = lax.scan(
        one_step, start_state, (key_steps, value_steps, jnp.arange(step_count, dtype=jnp.int32))
    )
    early_out = restore(outcome[0], local_kv, group_size, half_rows)
    late_out = restore(outcome[1], local_kv, group_size, half_rows)
    return jnp.concatenate([early_out, late_out], axis=0)


def solution(mesh):
    in_specs = (
        P("ctx", "head"),
        P("head", None),
        P("ctx", None),
        P("ctx", None),
        P("ctx", "head"),
        P("ctx", "head"),
        P("ctx", "head"),
        P(None, "head"),
        P(None, "head"),
        P(None, "head"),
    )
    out_specs = P("ctx", "head")
    return jax.shard_map(
        on_device, mesh=mesh, in_specs=in_specs, out_specs=out_specs, check_vma=False
    )
```

profile of v0, /device:TPU:229, one launch (start us, length us, event | category | flops | bytes accessed | tf_op | source)
XLA Modules:
  0.0 465.1 jit_solution(14019873165633874528)
XLA Ops:
  12.8 43.8 %all-reduce.2.cloned.1.call-done = f32[128,768]{1,0:T(8,128)} async-done(((f32[128,768]{1,0:T(8,128)}), f32[128,768]{1,0:T(8,128)}) %all-reduce.2.cloned.1.call-update) | async-done | bytes 393232 | tf_op jit(solution)/shard_map/psum | solution.py:91
  70.0 71.8 %all-gather.3.cloned.1.call-done = bf16[8192,256]{0,1:T(8,128)(2,1)} async-done(((bf16[128,256]{0,1:T(8,128)(2,1)}), bf16[8192,256]{0,1:T(8,128)(2,1)}) %all-gather.3.cloned.1.call-update) | async-done | bytes 4194320 | tf_op jit(solution)/shard_map/all_gather | solution.py:120
  141.8 6.0 %copy.45 = bf16[32,8,16,512]{3,2,1,0:T(8,128)(2,1)} copy(bf16[32,8,16,512]{3,1,2,0:T(8,128)(2,1)} %bitcast.58) | data formatting | bytes 8388608
  147.8 7.9 %copy.38 = bf16[16,512,2,128]{3,1,2,0:T(8,128)(2,1)} copy(bf16[16,512,2,128]{1,0,3,2:T(8,128)(2,1)} %bitcast.54) | data formatting | bytes 8388608
  155.7 65.0 %all-gather.5.cloned.1.call-done = bf16[8192,256]{1,0:T(8,128)(2,1)} async-done(((bf16[128,256]{1,0:T(8,128)(2,1)}), bf16[8192,256]{1,0:T(8,128)(2,1)}) %all-gather.5.cloned.1.call-update) | async-done | bytes 4194320 | tf_op jit(solution)/shard_map/all_gather | solution.py:121
  220.7 7.0 %reshape.175 = bf16[16,512,2,128]{3,2,1,0:T(2,128)(2,1)} reshape(bf16[8192,256]{1,0:T(8,128)(2,1)} %all-gather.5.cloned.1.call-done) | data formatting | bytes 8388608 | tf_op jit(solution)/shard_map/reshape | solution.py:126
  229.4 226.2 %while.23 = (s32[]{:T(128)}, f32[2,512]{1,0:T(2,128)S(1)}, f32[2,512]{1,0:T(2,128)S(1)}, f32[2,512,128]{2,1,0:T(8,128)}, f32[2,512]{1,0:T(2,128)S(1)}, /*index=5...) while((s32[]{:T(128)}, f32[2,512]{1,0:T(2,128)S(1)}, ...), condition=%wide.region_13.14_spmd.clone, body=%wide.region_4.13_spmd.clone.sunk | while | flops 551555584 | bytes 30563460 | solution.py:166
  239.1 4.4 conditional.7
  248.8 4.4 conditional.6
  253.2 4.4 conditional.7
  263.0 4.4 conditional.6
  267.4 4.4 conditional.7
  277.1 4.4 conditional.6
  281.5 4.4 conditional.7
  291.3 4.4 conditional.6
  295.7 4.4 conditional.7
  309.8 4.4 conditional.7
  319.5 4.4 conditional.6
  323.9 4.4 conditional.7
  333.7 4.4 conditional.6
  338.1 4.4 conditional.7
  347.8 4.4 conditional.6
  352.2 4.4 conditional.7
  362.0 4.4 conditional.6
  366.4 4.4 conditional.7
  376.1 4.4 conditional.6
  380.5 4.4 conditional.7
  394.6 4.4 conditional.7
  408.8 4.4 conditional.7
  422.9 4.4 conditional.7
  437.1 4.4 conditional.7
  451.2 4.4 conditional.7
  (604 shorter events, 249.5 us)
Async XLA Ops:
  6.5 4.3 copy-start.9
  6.5 4.3 copy-start.10
  6.5 50.1 %all-reduce.2.cloned.1.call-start = ((), (), s32[]{:S(2)}) async-start(), calls=%async_computation | async-start | bytes 786432 | tf_op jit(solution)/shard_map/psum | solution.py:91
  10.8 131.0 %all-gather.3.cloned.1.call-start = ((), (), s32[]{:S(2)}) async-start(), calls=%async_computation.1 | async-start | bytes 4259840 | tf_op jit(solution)/shard_map/all_gather | solution.py:120
  62.5 158.2 %all-gather.5.cloned.1.call-start = ((), (), s32[]{:S(2)}) async-start(), calls=%async_computation.2 | async-start | bytes 4259840 | tf_op jit(solution)/shard_map/all_gather | solution.py:121
  249.1 2.2 copy-start.1
  249.2 2.2 copy-start.5
  263.3 2.2 copy-start.1
  263.3 2.2 copy-start.5
  277.4 2.2 copy-start.1
  277.4 2.2 copy-start.5
  291.6 2.2 copy-start.1
  291.6 2.2 copy-start.5
  305.7 2.2 copy-start.1
  305.7 2.2 copy-start.5
  319.8 2.2 copy-start.1
  319.9 2.2 copy-start.5
  334.0 2.2 copy-start.1
  334.0 2.2 copy-start.5
  348.1 2.2 copy-start.1
  348.1 2.2 copy-start.5
  362.3 2.2 copy-start.1
  362.3 2.2 copy-start.5
  376.4 2.2 copy-start.1
  376.4 2.2 copy-start.5
  390.5 2.2 copy-start.1
  390.5 2.2 copy-start.5
  404.7 2.2 copy-start.1
  404.7 2.2 copy-start.5
  418.8 2.2 copy-start.1
  433.0 2.2 copy-start.1
  433.0 2.2 copy-start.5
  (72 other events, 112.5 us)
Sparse Core Ops, SparseCore 0:
  10.9 45.6 all-reduce.1
  62.6 79.1 all-gather.2
  145.0 75.6 all-gather.4
where the time goes:
time: 468 us; the launch traced here: 465 us
  waiting for transfers between devices  181 us (39%)
  local copies, waits for them, and re-layouts  114 us (24%)
  matrix products  92.2 us (20%)
  other arithmetic  33.7 us (7%)
  loops' own time  31.7 us (7%)
  between operations  13.3 us (3%)
    all_gather x1, waiting for transfers between devices, on_device(): key_piece = lax.all_gather(keys, 'ctx', axis=0, tiled=True)  71.8 us
    all_gather x1, waiting for transfers between devices, on_device(): value_piece = lax.all_gather(values, 'ctx', axis=0, tiled=True)  65 us
    dot_general x32, matrix products, compute(): jnp.einsum('gqd,kgd->gqk', query_rows, key_block, preferred_element_type=...  50.2 us
    psum x1, waiting for transfers between devices, on_device(): low_rank = lax.psum(partial_low, 'head')  43.8 us
    dot_general x32, matrix products, compute(): jnp.einsum('gqk,kgd->gqd', expo.astype(jnp.bfloat16), value_block, prefer...  34.6 us
    another operation x1, loops' own time, on_device(): lax.scan(one_step, start_state, (key_steps, value_steps, jnp.arange(step_...  29.4 us
    squeeze x16, local copies, waits for them, and re-layouts, on_device(): lax.scan(one_step, start_state, (key_steps, value_steps, jnp.arange(step_...  28.1 us
    dynamic_slice x32, local copies, waits for them, and re-layouts, on_device(): lax.scan(one_step, start_state, (key_steps, value_steps, jnp.arange(step_...  27.4 us
  transfers between devices with their start and end apart: 3, of which 3 were waited for; matrix products, arithmetic and copies ran while one was open for 5% of the time, Pallas kernels for 0%

commit v1 on v0

v1 whole, which is shorter than its diff:
```python
import functools
import math

import jax
import jax.numpy as jnp
from jax import lax
from jax.experimental import pallas as pl
from jax.experimental.pallas import tpu as pltpu
from jax.sharding import PartitionSpec as P

HD = 128
ADAPTERS = 8
RANK = 32
SPAN = ADAPTERS * RANK
ROWS = 128
GROUP = 8
ZS, XS, YS = 8, 4, 4
BLOCK = 2 * ROWS
SLAB = XS * BLOCK

rope_base = 500000.0
floor_value = -1e30
FACTOR = math.log2(math.e) / math.sqrt(HD)
VMEM_LIMIT = 40 * 1024 * 1024


def device(z, x, core, y):
    return (((z % ZS) * XS + x % XS) * 2 + core) * YS + y


def send(array, move):
    pairs = []
    for z in range(ZS):
        for x in range(XS):
            for core in range(2):
                for y in range(YS):
                    pairs.append((device(z, x, core, y), device(*move(z, x, core, y))))
    return lax.ppermute(array, ("ctx", "head"), pairs)


def swap_cores(array):
    return send(array, lambda z, x, core, y: (z, x, 1 - core, y))


def turn(raw, cosine, sine):
    return raw * cosine + pltpu.roll(raw, HD // 2, 1) * sine


def kv_kernel(core_ref, low_ref, more_ref, coef_ref, upk_ref, upv_ref, kb_ref, vb_ref, cos_ref, sin_ref, kv_ref, gq_ref):
    core = core_ref[0]
    coef = coef_ref[...]

    def gated(part):
        cols = slice(part * SPAN, (part + 1) * SPAN)
        return ((low_ref[:, cols] + more_ref[:, cols]) * coef).astype(jnp.bfloat16)

    gq_ref[...] = gated(0)
    key_raw = kb_ref[...].astype(jnp.float32) + jnp.dot(gated(1), upk_ref[...], preferred_element_type=jnp.float32)
    value = vb_ref[...].astype(jnp.float32) + jnp.dot(gated(2), upv_ref[...], preferred_element_type=jnp.float32)
    cosine, sine = cos_ref[...], sin_ref[...]
    keys = [turn(key_raw[:, h * HD : (h + 1) * HD], cosine, sine) for h in range(2)]
    values = [value[:, h * HD : (h + 1) * HD] for h in range(2)]
    first = core == 0
    kv_ref[0, :, :HD] = jnp.where(first, keys[0], keys[1]).astype(jnp.bfloat16)
    kv_ref[1, :, :HD] = jnp.where(first, keys[1], keys[0]).astype(jnp.bfloat16)
    kv_ref[0, :, HD:] = jnp.where(first, values[0], values[1]).astype(jnp.bfloat16)
    kv_ref[1, :, HD:] = jnp.where(first, values[1], values[0]).astype(jnp.bfloat16)


def q_kernel(core_ref, gq_ref, upq_ref, qb_ref, cos_ref, sin_ref, mine_ref, other_ref):
    core = core_ref[0]
    cosine, sine = cos_ref[...], sin_ref[...]
    gq = gq_ref[...]
    for target, group in ((other_ref, 1 - core), (mine_ref, core)):
        for j in range(GROUP):
            cols = pl.ds(pl.multiple_of((group * GROUP + j) * HD, HD), HD)
            raw = qb_ref[:, cols].astype(jnp.float32) + jnp.dot(
                gq, upq_ref[:, cols], preferred_element_type=jnp.float32
            )
            target[:, j * HD : (j + 1) * HD] = turn(raw, cosine, sine).astype(jnp.bfloat16)


def query_tile(qo_ref, qr_ref, g):
    cols = pl.ds(pl.multiple_of(g * HD, HD), HD)
    return jnp.concatenate([qo_ref[:, cols], qr_ref[:, cols]], axis=0)


def scores_of(query, keys):
    return lax.dot_general(query, keys, (((1,), (1,)), ((), ())), preferred_element_type=jnp.float32)


def pieces(array):
    return [array[:, j * HD : (j + 1) * HD] for j in range(array.shape[1] // HD)]


def weigh(parts, top, values):
    expo = [jnp.exp2(part * FACTOR - top) for part in parts]
    total = functools.reduce(jnp.add, expo)
    weights = jnp.concatenate([e.astype(jnp.bfloat16) for e in expo], axis=1)
    return total, jnp.dot(weights, values, preferred_element_type=jnp.float32)


def first_kernel(base_ref, qo_ref, qr_ref, kv_ref, top_ref, total_ref, acc_ref):
    row = lax.broadcasted_iota(jnp.int32, (ROWS, HD), 0)
    lane = lax.broadcasted_iota(jnp.int32, (ROWS, HD), 1)
    gap = jnp.concatenate([row - lane + base_ref[8], row - lane + base_ref[9]], axis=0)

    def body(g, carry):
        query = query_tile(qo_ref, qr_ref, g)
        scores = scores_of(query, kv_ref[0, :, :HD])
        parts = [
            jnp.where(gap >= base_ref[j], part, floor_value) for j, part in enumerate(pieces(scores))
        ]
        best = jnp.max(functools.reduce(jnp.maximum, parts), axis=1, keepdims=True)
        top = jnp.broadcast_to(best * FACTOR, (BLOCK, HD))
        total, acc = weigh(parts, top, kv_ref[0, :, HD:])
        top_ref[g] = top
        total_ref[g] = total
        acc_ref[g] = acc
        return carry

    lax.fori_loop(0, GROUP, body, 0)


def update(qo_ref, qr_ref, keys, values, top_ref, total_ref, acc_ref, g):
    query = query_tile(qo_ref, qr_ref, g)
    parts = pieces(scores_of(query, keys))
    best = jnp.max(functools.reduce(jnp.maximum, parts), axis=1, keepdims=True)
    old = top_ref[g]
    top = jnp.maximum(old, best * FACTOR)
    shrink = jnp.exp2(old - top)
    total, acc = weigh(parts, top, values)
    top_ref[g] = top
    total_ref[g] = total_ref[g] * shrink + total
    acc_ref[g] = acc_ref[g] * shrink + acc


def next_kernel(flag_ref, qo_ref, qr_ref, near_ref, far_ref, top_in, total_in, acc_in, top_ref, total_ref, acc_ref):
    top_ref[...] = top_in[...]
    total_ref[...] = total_in[...]
    acc_ref[...] = acc_in[...]
    for index, kv in enumerate((near_ref, far_ref)):

        @pl.when(flag_ref[index] != 0)
        def _(kv=kv):
            def body(g, carry):
                keys, values = kv[0, :, :HD], kv[0, :, HD:]
                update(qo_ref, qr_ref, keys, values, top_ref, total_ref, acc_ref, g)
                return carry

            lax.fori_loop(0, GROUP, body, 0)


def last_kernel(flag_ref, qo_ref, qr_ref, near_ref, far_ref, top_in, total_in, acc_in, own_ref, other_ref, top_ref, total_ref, acc_ref):
    next_kernel(
        flag_ref, qo_ref, qr_ref, near_ref, far_ref, top_in, total_in, acc_in, top_ref, total_ref, acc_ref
    )
    for g in range(GROUP):
        total = jnp.sum(total_ref[g], axis=1, keepdims=True)
        out = (acc_ref[g] / total).astype(jnp.bfloat16)
        own_ref[:, g * HD : (g + 1) * HD] = out[:ROWS]
        other_ref[:, g * HD : (g + 1) * HD] = out[ROWS:]


def whole():
    return pl.BlockSpec(memory_space=pltpu.VMEM)


def scalars():
    return pl.BlockSpec(memory_space=pltpu.SMEM)


def call(kernel, n_in, outs, flops, scratch=()):
    return pl.pallas_call(
        kernel,
        out_shape=outs,
        in_specs=[scalars()] + [whole()] * n_in,
        out_specs=tuple(whole() for _ in outs),
        scratch_shapes=list(scratch),
        compiler_params=pltpu.CompilerParams(vmem_limit_bytes=VMEM_LIMIT),
        cost_estimate=pl.CostEstimate(flops=flops, bytes_accessed=4 << 20, transcendentals=0),
    )


def on_device(activations, adapter_down, adapter_ids, adapter_weight, query_base, key_base, value_base, up_query, up_key, up_value):
    ctx = lax.axis_index("ctx").astype(jnp.int32)
    z, x, core = ctx // (2 * XS), (ctx // 2) % XS, ctx % 2
    cores = core.reshape(1)
    f32, b16 = jnp.float32, jnp.bfloat16

    partial_low = jnp.dot(activations, adapter_down, preferred_element_type=f32)

    labels = jnp.arange(SPAN, dtype=jnp.int32) // RANK
    coef = jnp.zeros((ROWS, SPAN), f32)
    for j in range(adapter_ids.shape[1]):
        coef = coef + jnp.where(adapter_ids[:, j : j + 1] == labels[None, :], adapter_weight[:, j : j + 1], 0.0)
    positions = (ctx * ROWS + jnp.arange(ROWS, dtype=jnp.int32)).astype(f32)
    inverse = jnp.exp(jnp.arange(HD // 2, dtype=f32) * (-2.0 * math.log(rope_base) / HD))
    angles = positions[:, None] * jnp.concatenate([inverse, inverse])[None, :]
    cosine = jnp.cos(angles)
    sign = jnp.where(jnp.arange(HD) < HD // 2, -1.0, 1.0).astype(f32)
    sine = jnp.sin(angles) * sign[None, :]

    one = send(partial_low, lambda z, x, c, y: (z, x, c, y ^ (1 if c == 0 else 3)))
    low = partial_low + one
    two = send(low, lambda z, x, c, y: (z, x, c, y ^ (3 if c == 0 else 1)))

    kv, gated_query = call(
        kv_kernel,
        9,
        (jax.ShapeDtypeStruct((2, ROWS, 2 * HD), b16), jax.ShapeDtypeStruct((ROWS, SPAN), b16)),
        1 << 27,
    )(cores, low, two, coef, up_key, up_value, key_base, value_base, cosine, sine)

    got = send(kv, lambda z, x, c, y: (z, x ^ (1 if c == 0 else 3), c, y))
    pair = jnp.concatenate([kv, got], axis=1)
    far_pair = send(pair, lambda z, x, c, y: (z, x ^ (3 if c == 0 else 1), c, y))
    half = jnp.concatenate([pair, far_pair], axis=1)
    rest = swap_cores(half)
    slab = jnp.concatenate([half, rest[::-1]], axis=1)

    half_shape = jax.ShapeDtypeStruct((ROWS, GROUP * HD), b16)
    q_own, q_other = call(q_kernel, 5, (half_shape, half_shape), 1 << 29)(
        cores, gated_query, up_query, query_base, cosine, sine
    )
    q_rest = swap_cores(q_other)

    state_shape = (jax.ShapeDtypeStruct((GROUP, BLOCK, HD), f32),) * 3
    step_x = jnp.where(core == 0, 1, 3)
    own_x = jnp.stack([x, x ^ step_x, x ^ (4 - step_x), x ^ 2])
    rest_x = jnp.stack([x, x ^ (4 - step_x), x ^ step_x, x ^ 2])
    bases = jnp.concatenate(
        [
            (own_x - x) * BLOCK + core * ROWS,
            (rest_x - x) * BLOCK + (1 - core) * ROWS,
            jnp.stack([core * ROWS, (1 - core) * ROWS]),
        ]
    ).astype(jnp.int32)
    state = call(first_kernel, 3, state_shape, 1 << 32)(bases, q_own, q_rest, slab)

    moving = slab
    for step in range(1, 4):
        moving = send(moving, lambda z, x, c, y: (z + (1 if c == 0 else -1), x, c, y))
        swapped = swap_cores(moving[1:])
        below = (z >= step).astype(jnp.int32)
        wrapped = (z + step >= ZS).astype(jnp.int32)
        flags = jnp.where(core == 0, jnp.stack([below, wrapped]), jnp.stack([wrapped, below]))
        state = call(next_kernel, 7, state_shape, 1 << 33)(flags, q_own, q_rest, moving, swapped, *state)
    ends = send(moving[:, : SLAB // 2], lambda z, x, c, y: (z + (1 if c == 0 else -1), x, c, y))
    swapped = swap_cores(ends[1:])
    flags = jnp.stack([z >= ZS // 2, z >= ZS // 2]).astype(jnp.int32)
    own, other = call(
        last_kernel,
        7,
        (half_shape, half_shape),
        1 << 32,
        scratch=[pltpu.VMEM((GROUP, BLOCK, HD), f32)] * 3,
    )(flags, q_own, q_rest, ends, swapped, *state)
    back = swap_cores(other)
    return jnp.concatenate([jnp.where(core == 0, own, back), jnp.where(core == 0, back, own)], axis=1)


def solution(mesh):
    in_specs = (
        P("ctx", "head"),
        P("head", None),
        P("ctx", None),
        P("ctx", None),
        P("ctx", "head"),
        P("ctx", "head"),
        P("ctx", "head"),
        P(None, "head"),
        P(None, "head"),
        P(None, "head"),
    )
    return jax.shard_map(on_device, mesh=mesh, in_specs=in_specs, out_specs=P("ctx", "head"), check_vma=False)
```

time: 468 us -> 138 us (0.29)
  the two profiles are of different devices: /device:TPU:229 before, /device:TPU:248 now
where the time goes in v1:
time: 138 us; the launch traced here: 135 us
  Pallas kernels  51 us (37%)
  waiting for transfers between devices  46.5 us (34%)
  local copies, waits for them, and re-layouts  18.6 us (13%)
  starting transfers between devices  11.5 us (8%)
  other arithmetic  4.96 us (4%)
  matrix products  2.37 us (2%)
    ppermute x15, waiting for transfers between devices, send(): return lax.ppermute(array, ('ctx', 'head'), pairs)  46.5 us
    pallas_call x3, Pallas kernels, on_device(): call(next_kernel, 7, state_shape, 1 << 33)  34 us
    unnamed x42, local copies, waits for them, and re-layouts  13.8 us
    ppermute x15, starting transfers between devices, send(): return lax.ppermute(array, ('ctx', 'head'), pairs)  11.5 us
    pallas_call x1, Pallas kernels, on_device(): call(last_kernel, 7, (half_shape, half_shape), 1 << 32, scratch=[pltpu.VM...  8.69 us
    pallas_call x1, Pallas kernels, on_device(): call(first_kernel, 3, state_shape, 1 << 32)(bases, q_own, q_rest, slab)  5.73 us
  transfers between devices with their start and end apart: 15, of which 8 were waited for; matrix products, arithmetic and copies ran while one was open for 3% of the time, Pallas kernels for 30%

profile of v1, /device:TPU:248, one launch (start us, length us, event | category | flops | bytes accessed | tf_op | source)
XLA Modules:
  0.0 135.3 jit_solution(9825069398030709244)
XLA Ops:
  0.0 1.9 %copy-done = bf16[2048,768]{1,0:T(8,128)(2,1)S(1)} copy-done((bf16[2048,768]{1,0:T(8,128)(2,1)S(1)}, bf16[2048,768]{1,0:T(8,128)(2,1)}, u32[]{:S(2)}) %copy-start) | copy-done | bytes 3145752
  1.9 2.4 %fusion.5 = f32[128,768]{1,0:T(8,128)} fusion(bf16[128,2048]{1,0:T(8,128)(2,1)} %param.10, bf16[2048,768]{1,0:T(8,128)(2,1)S(1)} %copy-done), kind=kOutput, calls=%fused_computation.33 | convolution fusion | flops 402653184 | bytes 4063232 | tf_op jit(solution)/shard_map/dot_general | solution.py:191
  5.1 1.0 fusion
  6.1 6.3 %collective-permute-done = f32[128,768]{1,0:T(8,128)} collective-permute-done((f32[128,768]{1,0:T(8,128)}, f32[128,768]{1,0:T(8,128)}, u32[]{:S(2)}, u32[]{:S(2)}) %collective-permute-start) | collective-permute-done | bytes 393248 | tf_op jit(solution)/shard_map/ppermute | solution.py:38
  12.4 1.2 add.52.low_ref
  14.7 8.0 %collective-permute-done.1.more_ref = f32[128,768]{1,0:T(8,128)} collective-permute-done((f32[128,768]{1,0:T(8,128)S(1)}, f32[128,768]{1,0:T(8,128)}, u32[]{:S(2)}, u32[]{:S(2)}) %collective-permute-start.1) | collective-permute-done | bytes 393248 | tf_op jit(solution)/shard_map/ppermute | solution.py:38
  27.9 1.2 shard_map.100
  29.1 1.6 %collective-permute-start.3 = (bf16[2,128,256]{2,1,0:T(8,128)(2,1)S(1)}, bf16[2,128,256]{2,1,0:T(8,128)(2,1)S(1)}, u32[]{:S(2)}, u32[]{:S(2)}) collective-permute-start(bf16[2,128,256]{2,1,0:T(8,128)(2,1)S(1)} %get-tuple-element.26), channel_id=1, source_target_pairs={{0,8},{1,9},{2,10},{3,11},{4,28},{5,29},{6,30},{7,31},{8,0},{9,1},... | collective-permute-start | bytes 393224 | tf_op jit(solution)/shard_map/ppermute | solution.py:38
  30.7 3.5 %collective-permute-done.3 = bf16[2,128,256]{2,1,0:T(8,128)(2,1)S(1)} collective-permute-done((bf16[2,128,256]{2,1,0:T(8,128)(2,1)S(1)}, bf16[2,128,256]{2,1,0:T(8,128)(2,1)S(1)}, u32[]{:S(2)}, u32[]{:S(2)}) %collective-permute-start.3) | collective-permute-done | bytes 131104 | tf_op jit(solution)/shard_map/ppermute | solution.py:38
  34.2 2.8 %collective-permute-start.4 = (bf16[2,256,256]{2,1,0:T(8,128)(2,1)S(1)}, bf16[2,256,256]{2,1,0:T(8,128)(2,1)S(1)}, u32[]{:S(2)}, u32[]{:S(2)}) collective-permute-start(bf16[2,256,256]{2,1,0:T(8,128)(2,1)S(1)} %pad_maximum_fusion.3), channel_id=1, source_target_pairs={{0,24},{1,25},{2,26},{3,27},{4,12},{5,13},{6,14},{7,15},{8,16},{9,... | collective-permute-start | bytes 786440 | tf_op jit(solution)/shard_map/ppermute | solution.py:38
  37.1 4.8 %collective-permute-done.4 = bf16[2,256,256]{2,1,0:T(8,128)(2,1)S(1)} collective-permute-done((bf16[2,256,256]{2,1,0:T(8,128)(2,1)S(1)}, bf16[2,256,256]{2,1,0:T(8,128)(2,1)S(1)}, u32[]{:S(2)}, u32[]{:S(2)}) %collective-permute-start.4) | collective-permute-done | bytes 262176 | tf_op jit(solution)/shard_map/ppermute | solution.py:38
  42.6 1.5 %collective-permute-done.5 = bf16[2,512,256]{2,1,0:T(8,128)(2,1)} collective-permute-done((bf16[2,512,256]{2,1,0:T(8,128)(2,1)S(1)}, bf16[2,512,256]{2,1,0:T(8,128)(2,1)}, u32[]{:S(2)}, u32[]{:S(2)}) %collective-permute-start.5) | collective-permute-done | bytes 524320 | tf_op jit(solution)/shard_map/ppermute | solution.py:38
  44.1 1.9 %rev.3 = bf16[2,512,256]{2,1,0:T(8,128)(2,1)} reverse(bf16[2,512,256]{2,1,0:T(8,128)(2,1)} %collective-permute-done.5), dimensions={0} | reverse | bytes 1048576 | tf_op jit(solution)/shard_map/rev | solution.py:220
  46.0 1.2 pad_maximum_fusion.kv_ref
  47.3 1.0 copy-done.2
  48.2 13.9 %collective-permute-done.6.near_ref = bf16[2,1024,256]{2,1,0:T(8,128)(2,1)} collective-permute-done((bf16[2,1024,256]{2,1,0:T(8,128)(2,1)S(1)}, bf16[2,1024,256]{2,1,0:T(8,128)(2,1)}, u32[]{:S(2)}, u32[]{:S(2)}) %collective-permute-start.6) | collective-permute-done | bytes 1048608 | tf_op jit(solution)/shard_map/ppermute | solution.py:38
  62.1 1.2 collective-permute-start.7
  63.6 1.2 copy-done.12
  64.8 1.0 copy-done.13
  65.9 1.3 shard_map.101
  68.0 1.1 slice.40
  69.8 7.5 %collective-permute-done.7.near_ref = bf16[2,1024,256]{2,1,0:T(8,128)(2,1)} collective-permute-done((bf16[2,1024,256]{2,1,0:T(8,128)(2,1)}, bf16[2,1024,256]{2,1,0:T(8,128)(2,1)}, u32[]{:S(2)}, u32[]{:S(2)}) %collective-permute-start.7) | collective-permute-done | bytes 1048608 | tf_op jit(solution)/shard_map/ppermute | solution.py:38
  77.3 2.4 %collective-permute-start.8 = (bf16[2,1024,256]{2,1,0:T(8,128)(2,1)}, bf16[2,1024,256]{2,1,0:T(8,128)(2,1)S(1)}, u32[]{:S(2)}, u32[]{:S(2)}) collective-permute-start(bf16[2,1024,256]{2,1,0:T(8,128)(2,1)} %collective-permute-done.7.near_ref), channel_id=1, source_target_pairs={{0,32},{1,33},{2,34},{3,35},{4,228},{5,229},{6,230},{7,231},{8,40}... | collective-permute-start | bytes 3145736 | tf_op jit(solution)/shard_map/ppermute | solution.py:38
  79.7 1.2 copy-done.3
  80.9 0.9 copy-done.17
  81.9 5.7 %shard_map.102 = (f32[8,256,128]{2,1,0:T(8,128)S(1)}, f32[8,256,128]{2,1,0:T(8,128)S(1)}, f32[8,256,128]{2,1,0:T(8,128)S(1)}) custom-call(s32[10]{0:T(128)S(1)} %pad_add_fusion.base_ref, bf16[128,1024]{1,0:T(8,128)(2,1)S(1)} %copy-done.17, bf16[128,1024]{1,0:T(8,128)(2,1)S(1)} %collective-permute-done.2.qr_ref, bf16[2,1024,256]{2,1,0:T(8,128)(2,1)S(1)} %copy-done.3), custom_call_target="tpu_custom_call" | custom-call | flops 4294967296 | bytes 4194304 | tf_op jit(solution)/shard_map/pallas_call | solution.py:239
  87.6 1.1 slice.39
  88.8 11.6 %shard_map.103 = (f32[8,256,128]{2,1,0:T(8,128)S(1)}, f32[8,256,128]{2,1,0:T(8,128)S(1)}, f32[8,256,128]{2,1,0:T(8,128)S(1)}) custom-call(s32[2]{0:T(128)S(1)} %broadcast_select_fusion.2.flag_ref, bf16[128,1024]{1,0:T(8,128)(2,1)S(1)} %copy-done.18, bf16[128,1024]{1,0:T(8,128)(2,1)S(1)} %collective-permute-done.2.qr_ref, ...), custom_call_target="tpu_custom_call" | custom-call | flops 8589934592 | bytes 4194304 | tf_op jit(solution)/shard_map/pallas_call | solution.py:248
  101.3 11.6 %shard_map.104 = (f32[8,256,128]{2,1,0:T(8,128)S(1)}, f32[8,256,128]{2,1,0:T(8,128)S(1)}, f32[8,256,128]{2,1,0:T(8,128)S(1)}) custom-call(s32[2]{0:T(128)S(1)} %broadcast_select_fusion.3.flag_ref, bf16[128,1024]{1,0:T(8,128)(2,1)S(1)} %copy-done.18, bf16[128,1024]{1,0:T(8,128)(2,1)S(1)} %collective-permute-done.2.qr_ref, ...), custom_call_target="tpu_custom_call" | custom-call | flops 8589934592 | bytes 4194304 | tf_op jit(solution)/shard_map/pallas_call | solution.py:248
  113.1 10.9 %shard_map.105 = (f32[8,256,128]{2,1,0:T(8,128)S(1)}, f32[8,256,128]{2,1,0:T(8,128)S(1)}, f32[8,256,128]{2,1,0:T(8,128)S(1)}) custom-call(s32[2]{0:T(128)S(1)} %broadcast_select_fusion.4.flag_ref, bf16[128,1024]{1,0:T(8,128)(2,1)S(1)} %copy-done.18, bf16[128,1024]{1,0:T(8,128)(2,1)S(1)} %collective-permute-done.2.qr_ref, ...), custom_call_target="tpu_custom_call" | custom-call | flops 8589934592 | bytes 4194304 | tf_op jit(solution)/shard_map/pallas_call | solution.py:248
  124.0 8.7 %shard_map.106 = (bf16[128,1024]{1,0:T(8,128)(2,1)S(1)}, bf16[128,1024]{1,0:T(8,128)(2,1)S(1)}) custom-call(s32[2]{0:T(128)S(1)} %add_convert_fusion.flag_ref, bf16[128,1024]{1,0:T(8,128)(2,1)S(1)} %copy-done.18, bf16[128,1024]{1,0:T(8,128)(2,1)S(1)} %collective-permute-done.2.qr_ref, bf16[2,512,256]{2,1,0:T(8,128)(2,1)S(1)} %collective-permute-done.9.near_ref, ...), custom_call_target="tpu_custom_call" | custom-call | flops 4294967296 | bytes 4194304 | tf_op jit(solution)/shard_map/pallas_call | solution.py:252
  133.3 1.2 collective-permute-done.14
  (74 shorter events, 12.4 us)
Async XLA Ops:
  0.0 1.9 %copy-start = (bf16[2048,768]{1,0:T(8,128)(2,1)S(1)}, bf16[2048,768]{1,0:T(8,128)(2,1)}, u32[]{:S(2)}) copy-start(bf16[2048,768]{1,0:T(8,128)(2,1)} %param.11) | copy-start | bytes 9437188
  0.0 5.0 %copy-start.20 = (s32[128,2]{0,1:T(2,128)S(1)}, s32[128,2]{0,1:T(2,128)}, u32[]{:S(2)}) copy-start(s32[128,2]{0,1:T(2,128)} %param.12) | copy-start | bytes 3076
  4.3 8.1 %collective-permute-start = (f32[128,768]{1,0:T(8,128)}, f32[128,768]{1,0:T(8,128)}, u32[]{:S(2)}, u32[]{:S(2)}) collective-permute-start(f32[128,768]{1,0:T(8,128)} %fusion.5), channel_id=1, source_target_pairs={{0,1},{1,0},{2,3},{3,2},{4,7},{5,6},{6,5},{7,4},{8,9},{9,8},{10,11... | collective-permute-start | bytes 1179656 | tf_op jit(solution)/shard_map/ppermute | solution.py:38
  13.5 9.2 %collective-permute-start.1 = (f32[128,768]{1,0:T(8,128)S(1)}, f32[128,768]{1,0:T(8,128)}, u32[]{:S(2)}, u32[]{:S(2)}) collective-permute-start(f32[128,768]{1,0:T(8,128)S(1)} %add.52.low_ref), channel_id=1, source_target_pairs={{0,3},{1,2},{2,1},{3,0},{4,5},{5,4},{6,7},{7,6},{8,11},{9,10},{10,... | collective-permute-start | bytes 1179656 | tf_op jit(solution)/shard_map/ppermute | solution.py:38
  22.7 0.8 copy-start.4
  24.4 0.9 copy-start.8
  25.3 0.9 copy-start.9
  26.2 0.8 copy-start.10
  29.1 12.8 %copy-start.1 = (bf16[2,128,256]{2,1,0:T(8,128)(2,1)}, bf16[2,128,256]{2,1,0:T(8,128)(2,1)S(1)}, u32[]{:S(2)}) copy-start(bf16[2,128,256]{2,1,0:T(8,128)(2,1)S(1)} %get-tuple-element.26) | copy-start | bytes 393220
  29.1 12.8 %copy-start.14 = (bf16[128,256]{1,0:T(8,128)(2,1)}, bf16[128,256]{1,0:T(8,128)(2,1)S(1)}, u32[]{:S(2)}) copy-start(bf16[128,256]{1,0:T(8,128)(2,1)S(1)} %get-tuple-element.23.gq_ref) | copy-start | bytes 196612
  29.1 5.1 %collective-permute-start.3 = (bf16[2,128,256]{2,1,0:T(8,128)(2,1)S(1)}, bf16[2,128,256]{2,1,0:T(8,128)(2,1)S(1)}, u32[]{:S(2)}, u32[]{:S(2)}) collective-permute-start(bf16[2,128,256]{2,1,0:T(8,128)(2,1)S(1)} %get-tuple-element.26), channel_id=1, source_target_pairs={{0,8},{1,9},{2,10},{3,11},{4,28},{5,29},{6,30},{7,31},{8,0},{9,1},... | collective-permute-start | bytes 393224 | tf_op jit(solution)/shard_map/ppermute | solution.py:38
  34.2 29.4 %copy-start.5 = (f32[128,128]{1,0:T(8,128)S(1)}, f32[128,128]{1,0:T(8,128)}, u32[]{:S(2)}) copy-start(f32[128,128]{1,0:T(8,128)} %get-tuple-element.43.sin_ref) | copy-start | bytes 196612
  34.2 29.4 %copy-start.7 = (f32[128,128]{1,0:T(8,128)S(1)}, f32[128,128]{1,0:T(8,128)}, u32[]{:S(2)}) copy-start(f32[128,128]{1,0:T(8,128)} %get-tuple-element.44.cos_ref) | copy-start | bytes 196612
  34.2 7.7 %collective-permute-start.4 = (bf16[2,256,256]{2,1,0:T(8,128)(2,1)S(1)}, bf16[2,256,256]{2,1,0:T(8,128)(2,1)S(1)}, u32[]{:S(2)}, u32[]{:S(2)}) collective-permute-start(bf16[2,256,256]{2,1,0:T(8,128)(2,1)S(1)} %pad_maximum_fusion.3), channel_id=1, source_target_pairs={{0,24},{1,25},{2,26},{3,27},{4,12},{5,13},{6,14},{7,15},{8,16},{9,... | collective-permute-start | bytes 786440 | tf_op jit(solution)/shard_map/ppermute | solution.py:38
  42.0 2.1 %collective-permute-start.5 = (bf16[2,512,256]{2,1,0:T(8,128)(2,1)S(1)}, bf16[2,512,256]{2,1,0:T(8,128)(2,1)}, u32[]{:S(2)}, u32[]{:S(2)}) collective-permute-start(bf16[2,512,256]{2,1,0:T(8,128)(2,1)S(1)} %pad_maximum_fusion.1), channel_id=1, source_target_pairs={{0,4},{1,5},{2,6},{3,7},{4,0},{5,1},{6,2},{7,3},{8,12},{9,13},{10,... | collective-permute-start | bytes 1572872 | tf_op jit(solution)/shard_map/ppermute | solution.py:38
  42.6 21.0 %copy-start.15 = (bf16[128,256]{1,0:T(8,128)(2,1)S(1)}, bf16[128,256]{1,0:T(8,128)(2,1)}, u32[]{:S(2)}) copy-start(bf16[128,256]{1,0:T(8,128)(2,1)} %copy-done.14) | copy-start | bytes 196612
  47.2 15.0 %collective-permute-start.6 = (bf16[2,1024,256]{2,1,0:T(8,128)(2,1)S(1)}, bf16[2,1024,256]{2,1,0:T(8,128)(2,1)}, u32[]{:S(2)}, u32[]{:S(2)}) collective-permute-start(bf16[2,1024,256]{2,1,0:T(8,128)(2,1)S(1)} %pad_maximum_fusion.kv_ref), channel_id=1, source_target_pairs={{0,32},{1,33},{2,34},{3,35},{4,228},{5,229},{6,230},{7,231},{8,40}... | collective-permute-start | bytes 3145736 | tf_op jit(solution)/shard_map/ppermute | solution.py:38
  47.3 1.0 copy-start.2
  62.1 15.1 %collective-permute-start.7 = (bf16[2,1024,256]{2,1,0:T(8,128)(2,1)}, bf16[2,1024,256]{2,1,0:T(8,128)(2,1)}, u32[]{:S(2)}, u32[]{:S(2)}) collective-permute-start(bf16[2,1024,256]{2,1,0:T(8,128)(2,1)} %collective-permute-done.6.near_ref), channel_id=1, source_target_pairs={{0,32},{1,33},{2,34},{3,35},{4,228},{5,229},{6,230},{7,231},{8,40}... | collective-permute-start | bytes 3145736 | tf_op jit(solution)/shard_map/ppermute | solution.py:38
  63.6 1.2 copy-start.12
  64.8 1.0 copy-start.13
  67.9 11.8 %collective-permute-start.2 = (bf16[128,1024]{1,0:T(8,128)(2,1)}, bf16[128,1024]{1,0:T(8,128)(2,1)S(1)}, u32[]{:S(2)}, u32[]{:S(2)}) collective-permute-start(bf16[128,1024]{1,0:T(8,128)(2,1)} %get-tuple-element.25), channel_id=1, source_target_pairs={{0,4},{1,5},{2,6},{3,7},{4,0},{5,1},{6,2},{7,3},{8,12},{9,13},{10,... | collective-permute-start | bytes 786440 | tf_op jit(solution)/shard_map/ppermute | solution.py:38
  69.1 19.7 %collective-permute-start.13 = (bf16[1,1024,256]{2,1,0:T(8,128)(2,1)S(1)}, bf16[1,1024,256]{2,1,0:T(8,128)(2,1)S(1)}, u32[]{:S(2)}, u32[]{:S(2)}) collective-permute-start(bf16[1,1024,256]{2,1,0:T(8,128)(2,1)S(1)} %slice.40), channel_id=1, source_target_pairs={{0,4},{1,5},{2,6},{3,7},{4,0},{5,1},{6,2},{7,3},{8,12},{9,13},{10,... | collective-permute-start | bytes 1572872 | tf_op jit(solution)/shard_map/ppermute | solution.py:38
  77.3 23.1 %collective-permute-start.8 = (bf16[2,1024,256]{2,1,0:T(8,128)(2,1)}, bf16[2,1024,256]{2,1,0:T(8,128)(2,1)S(1)}, u32[]{:S(2)}, u32[]{:S(2)}) collective-permute-start(bf16[2,1024,256]{2,1,0:T(8,128)(2,1)} %collective-permute-done.7.near_ref), channel_id=1, source_target_pairs={{0,32},{1,33},{2,34},{3,35},{4,228},{5,229},{6,230},{7,231},{8,40}... | collective-permute-start | bytes 3145736 | tf_op jit(solution)/shard_map/ppermute | solution.py:38
  79.7 1.2 copy-start.3
  80.9 0.9 copy-start.17
  81.9 6.9 %copy-start.18 = (bf16[128,1024]{1,0:T(8,128)(2,1)S(1)}, bf16[128,1024]{1,0:T(8,128)(2,1)}, u32[]{:S(2)}) copy-start(bf16[128,1024]{1,0:T(8,128)(2,1)} %copy-done.16) | copy-start | bytes 786436
  88.7 12.6 %collective-permute-start.12 = (bf16[1,1024,256]{2,1,0:T(8,128)(2,1)S(1)}, bf16[1,1024,256]{2,1,0:T(8,128)(2,1)S(1)}, u32[]{:S(2)}, u32[]{:S(2)}) collective-permute-start(bf16[1,1024,256]{2,1,0:T(8,128)(2,1)S(1)} %slice.39), channel_id=1, source_target_pairs={{0,4},{1,5},{2,6},{3,7},{4,0},{5,1},{6,2},{7,3},{8,12},{9,13},{10,... | collective-permute-start | bytes 1572872 | tf_op jit(solution)/shard_map/ppermute | solution.py:38
  100.4 12.6 %collective-permute-start.11 = (bf16[1,1024,256]{2,1,0:T(8,128)(2,1)S(1)}, bf16[1,1024,256]{2,1,0:T(8,128)(2,1)S(1)}, u32[]{:S(2)}, u32[]{:S(2)}) collective-permute-start(bf16[1,1024,256]{2,1,0:T(8,128)(2,1)S(1)} %slice.38), channel_id=1, source_target_pairs={{0,4},{1,5},{2,6},{3,7},{4,0},{5,1},{6,2},{7,3},{8,12},{9,13},{10,... | collective-permute-start | bytes 1572872 | tf_op jit(solution)/shard_map/ppermute | solution.py:38
  101.0 11.9 %collective-permute-start.9 = (bf16[2,512,256]{2,1,0:T(8,128)(2,1)S(1)}, bf16[2,512,256]{2,1,0:T(8,128)(2,1)S(1)}, u32[]{:S(2)}, u32[]{:S(2)}) collective-permute-start(bf16[2,512,256]{2,1,0:T(8,128)(2,1)S(1)} %slice.36), channel_id=1, source_target_pairs={{0,32},{1,33},{2,34},{3,35},{4,228},{5,229},{6,230},{7,231},{8,40}... | collective-permute-start | bytes 1572872 | tf_op jit(solution)/shard_map/ppermute | solution.py:38
  112.9 11.0 %collective-permute-start.10 = (bf16[1,512,256]{2,1,0:T(8,128)(2,1)S(1)}, bf16[1,512,256]{2,1,0:T(8,128)(2,1)S(1)}, u32[]{:S(2)}, u32[]{:S(2)}) collective-permute-start(bf16[1,512,256]{2,1,0:T(8,128)(2,1)S(1)} %slice.37), channel_id=1, source_target_pairs={{0,4},{1,5},{2,6},{3,7},{4,0},{5,1},{6,2},{7,3},{8,12},{9,13},{10,... | collective-permute-start | bytes 786440 | tf_op jit(solution)/shard_map/ppermute | solution.py:38
  132.7 1.7 %collective-permute-start.14 = (bf16[128,1024]{1,0:T(8,128)(2,1)S(1)}, bf16[128,1024]{1,0:T(8,128)(2,1)S(1)}, u32[]{:S(2)}, u32[]{:S(2)}) collective-permute-start(bf16[128,1024]{1,0:T(8,128)(2,1)S(1)} %get-tuple-element.40), channel_id=1, source_target_pairs={{0,4},{1,5},{2,6},{3,7},{4,0},{5,1},{6,2},{7,3},{8,12},{9,13},{10,... | collective-permute-start | bytes 786440 | tf_op jit(solution)/shard_map/ppermute | solution.py:38
  (4 other events, 3.1 us)
